TPU v7x, 32 devices: a whole 2x2x4 slice. The times are simulated.
32 devices in a mesh: groups: 2 (over y), ao: 8 (over z, core), aux: 2 (over x).
Axes of the slice: x: 2, y: 2, z: 4, core: 2. Of those that a mesh axis runs over, the one named last changes fastest.
Arguments:
- three_index: bfloat16 [64, 32, 128, 128], P(('groups', 'ao'), 'aux'), parts along dimension 0, may hold values from -0.25 to 0.25
- orbitals: bfloat16 [1024, 512], P('ao', 'groups'), parts along dimension 1, may hold values from -0.59765625 to 0.59765625
- partners: int32 [16, 4], P(('groups', 'ao')), parts along dimension 0, may hold values from 0 to 7, all different within a row
Outputs:
- exchange: float32 [64, 128, 128], P(('groups', 'ao'), 'aux'), parts along dimension 0
There are 2 independent parts, one for each index of `groups`. A program takes and returns all parts, laid end to end along the dimension named above; each array names one. Nothing has to cross between parts.
Inputs may be any that keep to these rules, and one draw needn't show every extreme that they name: `partners`: each row names 4 different blocks, and every block is named by some row.
All inputs are finite; a program needn't handle non-finite values.
Results may differ from a plain program's by a relative error of at most 0.0044.
Values may be sent and summed in bfloat16 or wider, within the bound.
A program may use at most 128 MiB of HBM per device.

v0:
```python
import jax
import jax.numpy as jnp
from jax import lax
from jax.sharding import PartitionSpec as P


def per_device(three_index, orbitals, partners):
    whole_coef = lax.all_gather(orbitals, "ao", axis=0, tiled=True)
    width = orbitals.shape[0]
    coef_blocks = whole_coef.reshape(-1, width, orbitals.shape[1])
    listed = partners[0]
    chosen = coef_blocks[listed]
    half = jnp.einsum(
        "pxab,pbi->xai", three_index, chosen, preferred_element_type=jnp.float32
    ).astype(jnp.bfloat16)
    piece = lax.all_gather(half[None], "ao", axis=0, tiled=True)
    count = piece.shape[0]
    products = jnp.einsum("xai,kxci->kac", half, piece, preferred_element_type=jnp.float32)
    picks = (listed[:, None] == jnp.arange(count, dtype=jnp.int32)[None, :]).astype(jnp.float32)
    partial_k = jnp.einsum("pk,kac->pac", picks, products)
    return lax.psum_scatter(partial_k, "aux", scatter_dimension=1, tiled=True)


def solution(mesh):
    placed = (P(("groups", "ao"), "aux", None, None), P("ao", "groups"), P(("groups", "ao"), None))
    return jax.shard_map(
        per_device,
        mesh=mesh,
        in_specs=placed,
        out_specs=P(("groups", "ao"), "aux", None),
        check_vma=False,
    )
```

profile of v0, /device:TPU:0, one launch (start us, length us, event | category | flops | bytes accessed | tf_op | source)
XLA Modules:
  0.0 147.3 jit_solution(15286433052512767513)
XLA Ops:
  6.5 0.0 copy-start
  6.5 0.0 all-gather.3.cloned.1.call-start
  6.5 16.9 %all_gather.6 = bf16[1024,256]{1,0:T(8,128)(2,1)S(1)} all-gather(bf16[128,256]{1,0:T(8,128)(2,1)} %param.4), channel_id=1, replica_groups=mesh['groups'=2,'ao'=8,'aux'=2] {'ao'}, dimensions={0}, use_global_device_ids=true | all-gather | bytes 589824 | tf_op jit(solution)/shard_map/all_gather | solution.py:8
  23.4 0.7 fusion.6
  24.1 0.6 gather_fusion
  24.7 0.0 copy-done
  24.7 0.8 bitcast_convert_fusion
  25.5 1.4 copy.11
  26.8 0.0 all-gather.3.cloned.1.call-update
  26.8 0.0 all-reduce.3.cloned.1.call-start
  26.9 83.2 %all-gather.3.cloned.1.call-done = bf16[128,128,256]{2,1,0:T(8,128)(2,1)} async-done(((bf16[16,128,256]{2,1,0:T(8,128)(2,1)}), bf16[128,128,256]{2,1,0:T(8,128)(2,1)}) %all-gather.3.cloned.1.call-update) | async-done | bytes 8388624 | tf_op jit(solution)/shard_map/all_gather | solution.py:16
  110.1 0.0 copy-start.1
  110.1 0.0 copy-start.2
  110.1 5.7 %convolution_bitcast_fusion = bf16[8,128,128]{1,2,0:T(8,128)(2,1)S(1)} fusion(bf16[8,16,128,256]{3,2,1,0:T(8,128)(2,1)} %bitcast.37, bf16[256,16,128]{2,0,1:T(8,128)(2,1)S(1)} %bitcast_convert_fusion), kind=kOutput, calls=%fused_computation.2 | convolution fusion | flops 1073741824 | bytes 9699328 | tf_op jit(solution)/shard_map/xai,kxci->kac/dot_general | solution.py:18
  115.8 0.2 copy.13
  116.0 0.0 copy-done.1
  116.0 1.0 fusion.3
  117.0 0.0 all-reduce.3.cloned.1.call-update
  117.0 0.0 copy-done.2
  117.1 0.6 dynamic-slice
  118.3 20.6 %all-reduce.3.cloned.1.call-done = f32[4,128,128]{2,0,1:T(4,128)} async-done(((f32[4,128,128]{2,0,1:T(4,128)}), f32[4,128,128]{2,0,1:T(4,128)}) %all-reduce.3.cloned.1.call-update) | async-done | bytes 262160
  138.9 0.9 constant_dynamic-slice_fusion
  139.8 0.7 copy.14
  (1 shorter events, 0.0 us)
Async XLA Ops:
  6.5 18.2 %copy-start = (bf16[4,16,128,128]{3,2,1,0:T(8,128)(2,1)S(1)}, bf16[4,16,128,128]{3,2,1,0:T(8,128)(2,1)}, u32[]{:S(2)}) copy-start(bf16[4,16,128,128]{3,2,1,0:T(8,128)(2,1)} %param.3) | copy-start | bytes 6291460
  6.5 103.6 %all-gather.3.cloned.1.call-start = ((), (), s32[]{:S(2)}) async-start(), calls=%async_computation | async-start | bytes 9437184 | tf_op jit(solution)/shard_map/all_gather | solution.py:16
  26.8 112.1 %all-reduce.3.cloned.1.call-start = ((), (), s32[]{:S(2)}) async-start(), calls=%async_computation.1 | async-start | bytes 524288
  110.1 5.9 %copy-start.1 = (s32[1,4]{1,0:T(1,128)S(1)}, s32[1,4]{1,0:T(1,128)}, u32[]{:S(2)}) copy-start(s32[1,4]{1,0:T(1,128)} %param.5) | copy-start | bytes 52
  110.1 7.0 %copy-start.2 = (u32[32]{0:T(128)S(1)}, u32[32]{0:T(128)}, u32[]{:S(2)}) copy-start(u32[32]{0:T(128)} %constant.8) | copy-start | bytes 388
Sparse Core Ops, SparseCore 0:
  27.0 83.0 all-gather.2
  117.2 21.7 all-reduce.2
where the time goes:
time: 148 us; the launch traced here: 147 us
  waiting for transfers between devices  104 us (70%)
  blocking collectives  16.9 us (11%)
  between operations  14.1 us (10%)
  matrix products  7.47 us (5%)
  local copies, waits for them, and re-layouts  4.29 us (3%)
    all_gather x1, waiting for transfers between devices, per_device(): piece = lax.all_gather(half[None], 'ao', axis=0, tiled=True)  83.2 us
    unnamed x3, waiting for transfers between devices  20.7 us
    all_gather x1, blocking collectives, per_device(): whole_coef = lax.all_gather(orbitals, 'ao', axis=0, tiled=True)  16.9 us
    dot_general x1, matrix products, per_device(): jnp.einsum('xai,kxci->kac', half, piece, preferred_element_type=jnp.float32)  5.74 us
  transfers between devices with their start and end apart: 2, of which 2 were waited for; matrix products, arithmetic and copies ran while one was open for 0% of the time, Pallas kernels for 0%

commit v1 on v0

v1 whole, which is shorter than its diff:
```python
import functools

import jax
import jax.numpy as jnp
from jax import lax
from jax.experimental import pallas as pl
from jax.experimental.pallas import tpu as pltpu
from jax.sharding import PartitionSpec as P

MESH = pl.DeviceIdType.MESH


def body(
    nao, nx,
    b_hbm, c_hbm, part, out,
    b_v, c_all, csel, pall, psm, hs, hbuf, kf, sx, rx, ks, kr, own,
    b_sem, c_loc, c_send, c_fwd, c_recv, p_send, p_recv, p_loc,
    h_send, h_recv, f_send, f_recv, x_send, x_recv, k_send, k_recv,
):
    me = lax.axis_index("ao")
    x = lax.axis_index("aux")
    nz = nao // 2
    z, c = me // 2, me % 2
    sib = z * 2 + 1 - c
    npair, npl, blk, _ = b_hbm.shape
    npz = npl // nz
    ra = blk // nx
    wide = c_hbm.shape[1]
    hw = wide // 2

    def remote(src, dst, send, recv, where):
        return pltpu.make_async_remote_copy(
            src_ref=src, dst_ref=dst, send_sem=send, recv_sem=recv,
            device_id=where, device_id_type=MESH,
        )

    loads = [pltpu.make_async_copy(b_hbm.at[p], b_v.at[p], b_sem.at[p]) for p in range(npair)]
    mine = pltpu.make_async_copy(c_hbm, c_all.at[me], c_loc)
    mine.start()
    for load in loads:
        load.start()

    barrier = pltpu.get_barrier_semaphore()
    for k in range(1, nao):
        pl.semaphore_signal(barrier, inc=1, device_id={"ao": (me + k) % nao}, device_id_type=MESH)
    for k in range(1, nx):
        pl.semaphore_signal(barrier, inc=1, device_id={"aux": (x + k) % nx}, device_id_type=MESH)
    pl.semaphore_wait(barrier, nao - 1 + nx - 1)

    far = [(z + nz // 2 + k) % nz for k in range(nz)]
    here = nz - nz // 2
    others = [k for k in range(nz) if k != here]
    sent = []
    for k in others:
        copy = remote(c_hbm, c_all.at[me], c_send.at[k], c_recv.at[me], {"ao": far[k] * 2 + c})
        copy.start()
        sent.append(copy)
    copy = remote(c_hbm, c_all.at[me], c_send.at[here], c_recv.at[me], {"ao": sib})
    copy.start()
    sent.append(copy)

    lane = lax.broadcasted_iota(jnp.int32, (8, 128), 1)
    row = jnp.zeros((8, 128), jnp.int32)
    for p in range(npair):
        row = jnp.where(lane == p, part[0, p], row)
    myrow = pall.at[pl.ds(pl.multiple_of(me * 8, 8), 8)]
    myrow[...] = row
    for k in range(1, nao):
        copy = remote(myrow, myrow, p_send.at[k], p_recv.at[me], {"ao": (me + k) % nao})
        copy.start()
        sent.append(copy)

    def arrived(ref, sem):
        remote(ref, ref, sem, sem, {"ao": sib}).wait_recv()

    for k in others[::-1]:
        n = far[k] * 2 + c
        arrived(c_all.at[n], c_recv.at[n])
        copy = remote(c_all.at[n], c_all.at[n], c_fwd.at[k], c_recv.at[n], {"ao": sib})
        copy.start()
        sent.append(copy)
    for k in range(nz):
        n = far[k] * 2 + 1 - c
        arrived(c_all.at[n], c_recv.at[n])
    mine.wait()
    for load in loads:
        load.wait()
    for p in range(npair):
        csel[p * blk:(p + 1) * blk, :] = c_all[part[0, p]]

    for j in range(npz):
        for k in range(nz):
            q = far[k] * npz + j
            left = jnp.concatenate([b_v[p, q] for p in range(npair)], axis=1)
            half = jnp.dot(left, csel[...], preferred_element_type=jnp.float32).astype(jnp.bfloat16)
            hs[q, 0] = half[:, :hw]
            hs[q, 1] = half[:, hw:]
            if k == here:
                hbuf[x, j, me] = hs[q, c]
                copy = remote(hs.at[q, 1 - c], hbuf.at[x, j, me], h_send.at[q, 0], h_recv.at[j, me], {"ao": sib})
                copy.start()
                sent.append(copy)
                for d in range(1, nx):
                    copy = remote(
                        hbuf.at[x, j, me], hbuf.at[x, j, me], f_send.at[d, j, me], f_recv.at[x, j, me],
                        {"aux": (x + d) % nx},
                    )
                    copy.start()
            else:
                for cc in range(2):
                    copy = remote(
                        hs.at[q, cc], hbuf.at[x, j, me], h_send.at[q, cc], h_recv.at[j, me],
                        {"ao": far[k] * 2 + cc},
                    )
                    copy.start()
                    sent.append(copy)

    for k in range(1, nao):
        n = (me + k) % nao
        theirs = pall.at[pl.ds(pl.multiple_of(n * 8, 8), 8)]
        arrived(theirs, p_recv.at[n])
    to_smem = pltpu.make_async_copy(pall, psm, p_loc)
    to_smem.start()
    to_smem.wait()

    def add_up(xs, j, first):
        lhs = hbuf[xs, j, :, pl.ds(pl.multiple_of(x * ra, ra), ra), :].reshape(nao * ra, hw)

        def step(t, _):
            rhs = hbuf[xs, j, pl.ds(2 * t, 2)].reshape(2 * blk, hw)
            got = lax.dot_general(lhs, rhs, (((1,), (1,)), ((), ())), preferred_element_type=jnp.float32)
            if first:
                kf[2 * t] = got[:, :blk]
                kf[2 * t + 1] = got[:, blk:]
            else:
                kf[2 * t] += got[:, :blk]
                kf[2 * t + 1] += got[:, blk:]
            return 0

        lax.fori_loop(0, nao // 2, step, 0)

    def take_others(j):
        for d in range(1, nx):
            xs = (x + d) % nx

            def get(n, _):
                arrived(hbuf.at[xs, j, n], f_recv.at[xs, j, n])
                return 0

            lax.fori_loop(0, nao, get, 0)
            add_up(xs, j, False)

    for j in range(npz):
        def pass_on(t, _):
            n = (me + 1 + t) % nao
            arrived(hbuf.at[x, j, n], h_recv.at[j, n])
            for d in range(1, nx):
                remote(
                    hbuf.at[x, j, n], hbuf.at[x, j, n], f_send.at[d, j, n], f_recv.at[x, j, n],
                    {"aux": (x + d) % nx},
                ).start()
            return 0

        lax.fori_loop(0, nao - 1, pass_on, 0)
        add_up(x, j, j == 0)
        if j > 0:
            take_others(j - 1)
    take_others(npz - 1)

    def picked(m, p):
        return kf[psm[m * 8, p], pl.ds(pl.multiple_of(m * ra, ra), ra), :]

    for k in range(nz):
        for p in range(npair):
            sx[k, p] = picked(far[k] * 2 + 1 - c, p)
        copy = remote(sx.at[k], rx.at[k], x_send.at[k], x_recv.at[k], {"ao": sib})
        copy.start()
        sent.append(copy)
    for k in range(nz):
        arrived(rx.at[k], x_recv.at[k])
        for p in range(npair):
            value = picked(far[k] * 2 + c, p) + rx[k, p]
            if k == here:
                own[p] = value
            else:
                ks[k, p] = value.astype(jnp.bfloat16)
        if k != here:
            copy = remote(ks.at[k], kr.at[z], k_send.at[k], k_recv.at[z], {"ao": far[k] * 2 + c})
            copy.start()
            sent.append(copy)
    total = own[...]
    for k in others:
        arrived(kr.at[far[k]], k_recv.at[far[k]])
        total += kr[far[k]].astype(jnp.float32)
    out[...] = total

    for copy in sent:
        copy.wait_send()

    def left_over(n, _):
        for j in range(npz):
            for d in range(1, nx):
                remote(
                    hbuf.at[x, j, n], hbuf.at[x, j, n], f_send.at[d, j, n], f_recv.at[x, j, n],
                    {"aux": (x + d) % nx},
                ).wait_send()
        return 0

    lax.fori_loop(0, nao, left_over, 0)


def per_device(nao, nx, three_index, orbitals, partners):
    npair, npl, blk, _ = three_index.shape
    wide = orbitals.shape[1]
    nz = nao // 2
    npz = npl // nz
    ra = blk // nx
    hw = wide // 2
    bf, f32 = jnp.bfloat16, jnp.float32
    dma = pltpu.SemaphoreType.DMA
    return pl.pallas_call(
        functools.partial(body, nao, nx),
        out_shape=jax.ShapeDtypeStruct((npair, ra, blk), f32),
        in_specs=[
            pl.BlockSpec(memory_space=pl.ANY),
            pl.BlockSpec(memory_space=pl.ANY),
            pl.BlockSpec(memory_space=pltpu.SMEM),
        ],
        out_specs=pl.BlockSpec(memory_space=pltpu.VMEM),
        scratch_shapes=[
            pltpu.VMEM((npair, npl, blk, blk), bf),
            pltpu.VMEM((nao, blk, wide), bf),
            pltpu.VMEM((npair * blk, wide), bf),
            pltpu.VMEM((nao * 8, 128), jnp.int32),
            pltpu.SMEM((nao * 8, 128), jnp.int32),
            pltpu.VMEM((npl, 2, blk, hw), bf),
            pltpu.VMEM((nx, npz, nao, blk, hw), bf),
            pltpu.VMEM((nao, nao * ra, blk), f32),
            pltpu.VMEM((nz, npair, ra, blk), f32),
            pltpu.VMEM((nz, npair, ra, blk), f32),
            pltpu.VMEM((nz, npair, ra, blk), bf),
            pltpu.VMEM((nz, npair, ra, blk), bf),
            pltpu.VMEM((npair, ra, blk), f32),
            dma((npair,)), dma, dma((nz,)), dma((nz,)), dma((nao,)),
            dma((nao,)), dma((nao,)), dma,
            dma((npl, 2)), dma((npz, nao)), dma((nx, npz, nao)), dma((nx, npz, nao)),
            dma((nz,)), dma((nz,)), dma((nz,)), dma((nz,)),
        ],
        compiler_params=pltpu.CompilerParams(
            collective_id=0, has_side_effects=True, vmem_limit_bytes=56 * 1024 * 1024,
        ),
    )(three_index, orbitals, partners)


def solution(mesh):
    placed = (P(("groups", "ao"), "aux", None, None), P("ao", "groups"), P(("groups", "ao"), None))
    return jax.shard_map(
        functools.partial(per_device, mesh.shape["ao"], mesh.shape["aux"]),
        mesh=mesh,
        in_specs=placed,
        out_specs=P(("groups", "ao"), "aux", None),
        check_vma=False,
    )
```

time: 148 us -> 59.8 us (0.40)
  waiting for transfers between devices: 104 us -> 0 us
  Pallas kernels: 0 us -> 58 us
  blocking collectives: 16.9 us -> 0 us
  between operations: 14.1 us -> 0.01 us
  matrix products: 7.47 us -> 0 us
  local copies, waits for them, and re-layouts: 4.29 us -> 1.57 us
    all_gather x1 -> x0, waiting for transfers between devices: 83.2 us -> none  [per_device(): piece = lax.all_gather(half[None], 'ao', axis=0, tiled=True)]
    pallas_call x0 -> x1, Pallas kernels: none -> 58 us  [per_device(): pl.pallas_call(functools.partial(body, nao, nx), out_shape=jax.ShapeDtype...]
    unnamed x3 -> x0, waiting for transfers between devices: 20.7 us -> none
    all_gather x1 -> x0, blocking collectives: 16.9 us -> none  [per_device(): whole_coef = lax.all_gather(orbitals, 'ao', axis=0, tiled=True)]
    dot_general x3 -> x0, matrix products: 7.47 us -> none  [the longest x1 5.74 us: per_device(): jnp.einsum('xai,kxci->kac', half, piece, preferred_element_type=jnp.float32)]
  transfers between devices with their start and end apart: 2 -> 0, of which waited for: 2 -> 0; matrix products, arithmetic and copies ran while one was open for 0% -> 0% of each run, Pallas kernels for 0% -> 0%
where the time goes in v1:
time: 59.8 us; the launch traced here: 59.6 us
  Pallas kernels  58 us (97%)
  local copies, waits for them, and re-layouts  1.57 us (3%)
    pallas_call x1, Pallas kernels, per_device(): pl.pallas_call(functools.partial(body, nao, nx), out_shape=jax.ShapeDtype...  58 us
    unnamed x1, local copies, waits for them, and re-layouts  1.57 us

profile of v1, /device:TPU:0, one launch (start us, length us, event | category | flops | bytes accessed | tf_op | source)
XLA Modules:
  0.0 59.6 jit_solution(1410336877068601992)
XLA Ops:
  0.0 58.0 %shard_map.37 = f32[4,64,128]{2,1,0:T(8,128)} custom-call(bf16[4,16,128,128]{3,2,1,0:T(8,128)(2,1)} %b_hbm.1, bf16[128,256]{1,0:T(8,128)(2,1)} %c_hbm.1, s32[1,4]{1,0:T(1,128)} %part.1), custom_call_target="tpu_custom_call" | custom-call | tf_op jit(solution)/shard_map/pallas_call | solution.py:221
  58.0 1.6 %copy.5 = f32[4,64,128]{2,1,0:T(8,128)} copy(f32[4,64,128]{2,1,0:T(8,128)} %shard_map.37) | data formatting | bytes 262144

commit v2 on v0

v2 whole, which is shorter than its diff:
```python
import functools

import jax
import jax.numpy as jnp
from jax import lax
from jax.experimental import pallas as pl
from jax.experimental.pallas import tpu as pltpu
from jax.sharding import PartitionSpec as P

MESH = pl.DeviceIdType.MESH


def c_order(nz):
    return range(nz - 1, 0, -1)


def plan(npz, nz):
    out = list(dict.fromkeys([nz - 1, *range(1, nz - 1), 0]))
    back = list(dict.fromkeys([1, nz - 1, *range(2, nz - 1), 0]))
    steps = [("send", j, k) for j in range(npz) for k in out] + [("rows", 0, 0)]
    for j in range(npz):
        steps += [("pass", j, k) for k in back] + [("ship", j, 0)]
        if j > 0:
            steps += [("others", j - 1, 0)]
    return steps + [("lists", 0, 0), ("others", npz - 1, 0)]


def body(
    nao, nx,
    b_hbm, c_hbm, part, out,
    b_v, c_all, csel, pall, psm, hs, hsx, b_x, hbuf, kf, sx, rx, ks, kr, own,
    b_sem, c_loc, c_send, c_recv, s_send, s_recv, p_send, p_recv, p_loc,
    bx_send, bx_recv, h_send, h_recv, f_send, f_recv, x_send, x_recv, k_send, k_recv,
):
    me = lax.axis_index("ao")
    x = lax.axis_index("aux")
    nz = nao // 2
    z, c = me // 2, me % 2
    sib = z * 2 + 1 - c
    npair, npl, blk, _ = b_hbm.shape
    npz = npl // nz
    ra = blk // nx
    wide = c_hbm.shape[1]
    hw = wide // 2
    cuts = 2
    cr = blk // cuts

    def remote(src, dst, send, recv, where):
        return pltpu.make_async_remote_copy(
            src_ref=src, dst_ref=dst, send_sem=send, recv_sem=recv,
            device_id=where, device_id_type=MESH,
        )

    def arrived(ref, sem):
        remote(ref, ref, sem, sem, {"ao": sib}).wait_recv()

    def left(ref, sem):
        remote(ref, ref, sem, sem, {"ao": sib}).wait_send()

    met = []
    for k in range(nz):
        zk = z
        bit = 1
        while bit < nz:
            if k & bit:
                zk = zk + bit - 2 * bit * ((zk // bit) % 2)
            bit *= 2
        met.append(zk)

    mine = pltpu.make_async_copy(c_hbm, c_all.at[me], c_loc)
    mine.start()
    load = pltpu.make_async_copy(b_hbm, b_v, b_sem)
    load.start()

    barrier = pltpu.get_barrier_semaphore()
    pl.semaphore_signal(barrier, inc=1, device_id={"ao": sib}, device_id_type=MESH)
    for k in range(1, nx):
        pl.semaphore_signal(barrier, inc=1, device_id={"aux": (x + k) % nx}, device_id_type=MESH)

    for k in range(1, nz):
        pl.semaphore_signal(barrier, inc=1, device_id={"ao": met[k] * 2 + c}, device_id_type=MESH)
    pl.semaphore_wait(barrier, nx + nz - 1)

    for k in c_order(nz):
        for h in range(cuts):
            piece = pl.ds(h * cr, cr)
            remote(
                c_hbm.at[piece], c_all.at[me, piece], c_send, c_recv.at[k, h], {"ao": met[k] * 2 + c},
            ).start()
    remote(c_hbm, c_all.at[me], s_send, s_recv, {"ao": sib}).start()

    for d in range(1, nx):
        for p in range(npair):
            remote(
                b_hbm.at[p, pl.ds(z * npz, npz)], b_x.at[x, p], bx_send, bx_recv.at[x], {"aux": (x + d) % nx},
            ).start()

    for k in range(1, nz):
        for h in range(cuts):
            piece = c_all.at[met[k] * 2 + c, pl.ds(h * cr, cr)]
            arrived(piece, c_recv.at[k, h])
            remote(piece, piece, s_send, s_recv, {"ao": sib}).start()

    lane = lax.broadcasted_iota(jnp.int32, (8, 128), 1)
    row = jnp.zeros((8, 128), jnp.int32)
    for p in range(npair):
        row = jnp.where(lane == p, part[0, p], row)
    myrow = pall.at[pl.ds(pl.multiple_of(me * 8, 8), 8)]
    myrow[...] = row
    mine.wait()
    load.wait()
    arrived(c_all.at[pl.ds(0, nz)], s_recv)
    for p in range(npair):
        csel[p * blk:(p + 1) * blk, :] = c_all[part[0, p]]

    def pass_on(j, n, count):
        for d in range(1, nx):
            for i in range(count):
                piece = hbuf.at[x, j, n + i]
                remote(piece, piece, f_send.at[d], f_recv.at[x, j], {"aux": (x + d) % nx}).start()

    def transformed(blocks):
        rows = jnp.concatenate(blocks, axis=1)
        return jnp.dot(rows, csel[...], preferred_element_type=jnp.float32).astype(jnp.bfloat16)

    def send(j, k):
        q = met[k] * npz + j
        half = transformed([b_v[p, q] for p in range(npair)])
        hs[q, 0] = half[:, :hw]
        hs[q, 1] = half[:, hw:]
        if k == 0:
            hbuf[x, j, me] = hs[q, c]
            remote(hs.at[q, 1 - c], hbuf.at[x, j, me], h_send.at[1], h_recv.at[j, 0], {"ao": sib}).start()
        else:
            for cc in range(2):
                remote(
                    hs.at[q, cc], hbuf.at[x, j, me], h_send.at[0], h_recv.at[j, k], {"ao": met[k] * 2 + cc},
                ).start()


    def ship(j):
        for d in range(1, nx):
            xs = (x + d) % nx
            if j == 0:
                arrived(b_x.at[xs], bx_recv.at[xs])
            half = transformed([b_x[xs, p, j] for p in range(npair)])
            hsx[d, j, 0] = half[:, :hw]
            hsx[d, j, 1] = half[:, hw:]
            hbuf[xs, j, me] = hsx[d, j, c]
            remote(hsx.at[d, j, 1 - c], hbuf.at[xs, j, me], h_send.at[2], f_recv.at[xs, j], {"ao": sib}).start()

    def receive(j, k):
        if k == 0:
            arrived(hbuf.at[x, j, sib], h_recv.at[j, 0])
        else:
            arrived(hbuf.at[x, j, pl.ds(met[k] * 2, 2)], h_recv.at[j, k])
            pass_on(j, met[k] * 2, 2)

    def add_up(xs, j, first):
        lhs = hbuf[xs, j, :, pl.ds(pl.multiple_of(x * ra, ra), ra), :].reshape(nao * ra, hw)

        def step(t, _):
            rhs = hbuf[xs, j, pl.ds(2 * t, 2)].reshape(2 * blk, hw)
            got = lax.dot_general(lhs, rhs, (((1,), (1,)), ((), ())), preferred_element_type=jnp.float32)
            if first:
                kf[2 * t] = got[:, :blk]
                kf[2 * t + 1] = got[:, blk:]
            else:
                kf[2 * t] += got[:, :blk]
                kf[2 * t + 1] += got[:, blk:]
            return 0

        lax.fori_loop(0, nao // 2, step, 0)

    def take_others(j):
        for d in range(1, nx):
            xs = (x + d) % nx
            arrived(hbuf.at[xs, j, pl.ds(0, nao - 1)], f_recv.at[xs, j])
            add_up(xs, j, False)

    missing = [nz] * npz
    for kind, j, k in plan(npz, nz):
        if kind == "send":
            send(j, k)
        elif kind == "rows":
            for i in range(1, nao):
                remote(myrow, myrow, p_send, p_recv, {"ao": (me + i) % nao}).start()
        elif kind == "ship":
            ship(j)
        elif kind == "lists":
            arrived(pall.at[pl.ds(0, (nao - 1) * 8)], p_recv)
            to_smem = pltpu.make_async_copy(pall, psm, p_loc)
            to_smem.start()
            to_smem.wait()
        elif kind == "others":
            take_others(j)
        else:
            receive(j, k)
            missing[j] -= 1
            if missing[j] == 0:
                add_up(x, j, j == 0)


    def picked(m, p):
        return kf[psm[m * 8, p], pl.ds(pl.multiple_of(m * ra, ra), ra), :]

    for k in range(nz - 1, -1, -1):
        for p in range(npair):
            sx[k, p] = picked(met[k] * 2 + 1 - c, p)
        remote(sx.at[k], rx.at[k], x_send, x_recv.at[k], {"ao": sib}).start()
    for k in range(nz - 1, -1, -1):
        arrived(rx.at[k], x_recv.at[k])
        for p in range(npair):
            value = picked(met[k] * 2 + c, p) + rx[k, p]
            if k == 0:
                own[p] = value
            else:
                ks[k, p] = value.astype(jnp.bfloat16)
        if k > 0:
            remote(ks.at[k], kr.at[k], k_send, k_recv, {"ao": met[k] * 2 + c}).start()
    total = own[...]
    arrived(kr.at[pl.ds(1, nz - 1)], k_recv)
    for k in range(1, nz):
        total += kr[k].astype(jnp.float32)
    out[...] = total

    left(c_all.at[pl.ds(0, nz - 1)], c_send)
    left(c_all.at[pl.ds(0, nz)], s_send)
    left(pall.at[pl.ds(0, (nao - 1) * 8)], p_send)
    left(hs.at[pl.ds(0, npl - npz)], h_send.at[0])
    left(hs.at[pl.ds(0, npz), 0], h_send.at[1])
    left(hsx.at[pl.ds(1, nx - 1), :, 0], h_send.at[2])
    left(b_x.at[pl.ds(0, nx - 1)], bx_send)
    for d in range(1, nx):
        left(hbuf.at[x, :, pl.ds(0, nao - 2)], f_send.at[d])
    left(rx, x_send)
    left(ks.at[pl.ds(1, nz - 1)], k_send)


def per_device(nao, nx, three_index, orbitals, partners):
    npair, npl, blk, _ = three_index.shape
    wide = orbitals.shape[1]
    nz = nao // 2
    npz = npl // nz
    ra = blk // nx
    hw = wide // 2
    bf, f32 = jnp.bfloat16, jnp.float32
    dma = pltpu.SemaphoreType.DMA
    return pl.pallas_call(
        functools.partial(body, nao, nx),
        out_shape=jax.ShapeDtypeStruct((npair, ra, blk), f32),
        in_specs=[
            pl.BlockSpec(memory_space=pl.ANY),
            pl.BlockSpec(memory_space=pl.ANY),
            pl.BlockSpec(memory_space=pltpu.SMEM),
        ],
        out_specs=pl.BlockSpec(memory_space=pltpu.VMEM),
        scratch_shapes=[
            pltpu.VMEM((npair, npl, blk, blk), bf),
            pltpu.VMEM((nao, blk, wide), bf),
            pltpu.VMEM((npair * blk, wide), bf),
            pltpu.VMEM((nao * 8, 128), jnp.int32),
            pltpu.SMEM((nao * 8, 128), jnp.int32),
            pltpu.VMEM((npl, 2, blk, hw), bf),
            pltpu.VMEM((nx, npz, 2, blk, hw), bf),
            pltpu.VMEM((nx, npair, npz, blk, blk), bf),
            pltpu.VMEM((nx, npz, nao, blk, hw), bf),
            pltpu.VMEM((nao, nao * ra, blk), f32),
            pltpu.VMEM((nz, npair, ra, blk), f32),
            pltpu.VMEM((nz, npair, ra, blk), f32),
            pltpu.VMEM((nz, npair, ra, blk), bf),
            pltpu.VMEM((nz, npair, ra, blk), bf),
            pltpu.VMEM((npair, ra, blk), f32),
            dma, dma, dma, dma((nz, 2)), dma, dma, dma, dma, dma,
            dma, dma((nx,)), dma((3,)), dma((npz, nz)), dma((nx,)), dma((nx, npz)),
            dma, dma((nz,)), dma, dma,
        ],
        compiler_params=pltpu.CompilerParams(
            collective_id=0, has_side_effects=True, vmem_limit_bytes=56 * 1024 * 1024,
        ),
    )(three_index, orbitals, partners)


def solution(mesh):
    placed = (P(("groups", "ao"), "aux", None, None), P("ao", "groups"), P(("groups", "ao"), None))
    return jax.shard_map(
        functools.partial(per_device, mesh.shape["ao"], mesh.shape["aux"]),
        mesh=mesh,
        in_specs=placed,
        out_specs=P(("groups", "ao"), "aux", None),
        check_vma=False,
    )
```

time: 148 us -> 53.8 us (0.36)
  waiting for transfers between devices: 104 us -> 0 us
  Pallas kernels: 0 us -> 52.1 us
  blocking collectives: 16.9 us -> 0 us
  between operations: 14.1 us -> 0.01 us
  matrix products: 7.47 us -> 0 us
  local copies, waits for them, and re-layouts: 4.29 us -> 1.57 us
    all_gather x1 -> x0, waiting for transfers between devices: 83.2 us -> none  [per_device(): piece = lax.all_gather(half[None], 'ao', axis=0, tiled=True)]
    pallas_call x0 -> x1, Pallas kernels: none -> 52.1 us  [per_device(): pl.pallas_call(functools.partial(body, nao, nx), out_shape=jax.ShapeDtype...]
    unnamed x3 -> x0, waiting for transfers between devices: 20.7 us -> none
    all_gather x1 -> x0, blocking collectives: 16.9 us -> none  [per_device(): whole_coef = lax.all_gather(orbitals, 'ao', axis=0, tiled=True)]
    dot_general x3 -> x0, matrix products: 7.47 us -> none  [the longest x1 5.74 us: per_device(): jnp.einsum('xai,kxci->kac', half, piece, preferred_element_type=jnp.float32)]
  transfers between devices with their start and end apart: 2 -> 0, of which waited for: 2 -> 0; matrix products, arithmetic and copies ran while one was open for 0% -> 0% of each run, Pallas kernels for 0% -> 0%
where the time goes in v2:
time: 53.8 us; the launch traced here: 53.7 us
  Pallas kernels  52.1 us (97%)
  local copies, waits for them, and re-layouts  1.57 us (3%)
    pallas_call x1, Pallas kernels, per_device(): pl.pallas_call(functools.partial(body, nao, nx), out_shape=jax.ShapeDtype...  52.1 us
    unnamed x1, local copies, waits for them, and re-layouts  1.57 us

profile of v2, /device:TPU:0, one launch (start us, length us, event | category | flops | bytes accessed | tf_op | source)
XLA Modules:
  0.0 53.7 jit_solution(13304580618179947082)
XLA Ops:
  0.0 52.1 %shard_map.37 = f32[4,64,128]{2,1,0:T(8,128)} custom-call(bf16[4,16,128,128]{3,2,1,0:T(8,128)(2,1)} %b_hbm.1, bf16[128,256]{1,0:T(8,128)(2,1)} %c_hbm.1, s32[1,4]{1,0:T(1,128)} %part.1), custom_call_target="tpu_custom_call" | custom-call | tf_op jit(solution)/shard_map/pallas_call | solution.py:249
  52.1 1.6 %copy.5 = f32[4,64,128]{2,1,0:T(8,128)} copy(f32[4,64,128]{2,1,0:T(8,128)} %shard_map.37) | data formatting | bytes 262144

commit v3 on v2

--- a/solution.py
+++ b/solution.py
@@ -27,8 +27,8 @@
 
 def body(
     nao, nx,
-    b_hbm, c_hbm, part, out,
-    b_v, c_all, csel, pall, psm, hs, hsx, b_x, hbuf, kf, sx, rx, ks, kr, own,
+    b_hbm, c_hbm, part, own, rest,
+    b_v, c_all, csel, pall, psm, hs, hsx, b_x, hbuf, kf, sx, rx, ks, kr,
     b_sem, c_loc, c_send, c_recv, s_send, s_recv, p_send, p_recv, p_loc,
     bx_send, bx_recv, h_send, h_recv, f_send, f_recv, x_send, x_recv, k_send, k_recv,
 ):
@@ -218,11 +218,11 @@
                 ks[k, p] = value.astype(jnp.bfloat16)
         if k > 0:
             remote(ks.at[k], kr.at[k], k_send, k_recv, {"ao": met[k] * 2 + c}).start()
-    total = own[...]
     arrived(kr.at[pl.ds(1, nz - 1)], k_recv)
-    for k in range(1, nz):
+    total = kr[1].astype(jnp.float32)
+    for k in range(2, nz):
         total += kr[k].astype(jnp.float32)
-    out[...] = total
+    rest[...] = total
 
     left(c_all.at[pl.ds(0, nz - 1)], c_send)
     left(c_all.at[pl.ds(0, nz)], s_send)
@@ -246,15 +246,15 @@
     hw = wide // 2
     bf, f32 = jnp.bfloat16, jnp.float32
     dma = pltpu.SemaphoreType.DMA
-    return pl.pallas_call(
+    own, rest = pl.pallas_call(
         functools.partial(body, nao, nx),
-        out_shape=jax.ShapeDtypeStruct((npair, ra, blk), f32),
+        out_shape=[jax.ShapeDtypeStruct((npair, ra, blk), f32)] * 2,
         in_specs=[
             pl.BlockSpec(memory_space=pl.ANY),
             pl.BlockSpec(memory_space=pl.ANY),
             pl.BlockSpec(memory_space=pltpu.SMEM),
         ],
-        out_specs=pl.BlockSpec(memory_space=pltpu.VMEM),
+        out_specs=[pl.BlockSpec(memory_space=pltpu.VMEM)] * 2,
         scratch_shapes=[
             pltpu.VMEM((npair, npl, blk, blk), bf),
             pltpu.VMEM((nao, blk, wide), bf),
@@ -270,7 +270,6 @@
             pltpu.VMEM((nz, npair, ra, blk), f32),
             pltpu.VMEM((nz, npair, ra, blk), bf),
             pltpu.VMEM((nz, npair, ra, blk), bf),
-            pltpu.VMEM((npair, ra, blk), f32),
             dma, dma, dma, dma((nz, 2)), dma, dma, dma, dma, dma,
             dma, dma((nx,)), dma((3,)), dma((npz, nz)), dma((nx,)), dma((nx, npz)),
             dma, dma((nz,)), dma, dma,
@@ -279,6 +278,7 @@
             collective_id=0, has_side_effects=True, vmem_limit_bytes=56 * 1024 * 1024,
         ),
     )(three_index, orbitals, partners)
+    return own + rest
 
 
 def solution(mesh):

time: 53.8 us -> 54 us (level)
  other arithmetic: 0 us -> 1.64 us
  local copies, waits for them, and re-layouts: 1.57 us -> 0 us
    add x0 -> x1, other arithmetic: none -> 1.64 us  [per_device(): return own + rest]
    unnamed x1 -> x0, local copies, waits for them, and re-layouts: 1.57 us -> none
where the time goes in v3:
time: 54 us; the launch traced here: 53.8 us
  Pallas kernels  52.2 us (97%)
  other arithmetic  1.64 us (3%)
    pallas_call x1, Pallas kernels, per_device(): pl.pallas_call(functools.partial(body, nao, nx), out_shape=[jax.ShapeDtyp...  52.2 us
    add x1, other arithmetic, per_device(): return own + rest  1.64 us

profile of v3, /device:TPU:0, one launch (start us, length us, event | category | flops | bytes accessed | tf_op | source)
XLA Modules:
  0.0 53.8 jit_solution(5412631136428204653)
XLA Ops:
  0.0 52.2 %shard_map.37 = (f32[4,64,128]{2,1,0:T(8,128)}, f32[4,64,128]{2,1,0:T(8,128)}) custom-call(bf16[4,16,128,128]{3,2,1,0:T(8,128)(2,1)} %b_hbm.1, bf16[128,256]{1,0:T(8,128)(2,1)} %c_hbm.1, s32[1,4]{1,0:T(1,128)} %part.1), custom_call_target="tpu_custom_call" | custom-call | tf_op jit(solution)/shard_map/pallas_call | solution.py:249
  52.2 1.6 %add.3 = f32[4,64,128]{2,1,0:T(8,128)} add(f32[4,64,128]{2,1,0:T(8,128)} %get-tuple-element.7, f32[4,64,128]{2,1,0:T(8,128)} %get-tuple-element.8) | non-fusion elementwise | flops 32768 | bytes 393216 | tf_op jit(solution)/shard_map/add | solution.py:281
